TPU v7x, 256 devices: a whole 4x4x8 slice. The times are simulated.
256 devices in a mesh: gen: 32 (over y, x, core), beam: 8 (over z).
Axes of the slice: x: 4, y: 4, z: 8, core: 2. Of those that a mesh axis runs over, the one named last changes fastest.
Arguments:
- gen_showers: bfloat16 [32768, 256], P('gen'), may hold values from -12 to 12
- beam_showers: bfloat16 [16384, 256], P('beam'), may hold values from -6 to 6
- embed_weight: bfloat16 [256, 128], replicated, may hold values from -0.375 to 0.375
- eps_roster: float32 [4], replicated, may hold values from 0.04 to 0.08
Outputs:
- gen_potential: float32 [32768], P('gen')
- beam_potential: float32 [16384], P('beam')
- weight_grad: float32 [256, 128], replicated
All inputs are finite; a program needn't handle non-finite values.
Results may differ from a plain program's by a relative error of at most 0.03.
Values sent between devices are 32-bit elements; how exact they have to be, the bound alone decides.
No kernel may reach another device: no remote copies, remote signals or barrier semaphores. Data moves between devices by JAX's collectives and lax.ppermute only.
A program may use at most 64 MiB of HBM per device.

v0:
```python
import math
import jax
import jax.numpy as jnp
from jax import lax
from jax.sharding import PartitionSpec as P

SWEEPS = 4


def embed(showers, weight):
    act = jnp.tanh(jnp.dot(showers, weight, preferred_element_type=jnp.float32))
    return (act, act.astype(jnp.bfloat16))


def tile_cost(gen_emb, beam_emb, gen_sq, beam_sq):
    cross = lax.dot_general(
        gen_emb, beam_emb, (((1,), (1,)), ((), ())), preferred_element_type=jnp.float32
    )
    return gen_sq[:, None] + beam_sq[None, :] - 2.0 * cross


def row_lse(scores):
    top = lax.pmax(jnp.max(scores, axis=1), "beam")
    total = lax.psum(jnp.sum(jnp.exp(scores - top[:, None]), axis=1), "beam")
    return top + jnp.log(total)


def col_lse(scores):
    top = lax.pmax(jnp.max(scores, axis=0), "gen")
    total = lax.psum(jnp.sum(jnp.exp(scores - top[None, :]), axis=0), "gen")
    return top + jnp.log(total)


def transpose_dot(left, right):
    return lax.dot_general(
        left.astype(jnp.float32),
        right,
        (((0,), (0,)), ((), ())),
        precision=lax.Precision.HIGHEST,
        preferred_element_type=jnp.float32,
    )


def on_device(gen_showers, beam_showers, embed_weight, eps_roster):
    gen_act, gen_emb = embed(gen_showers, embed_weight)
    beam_act, beam_emb = embed(beam_showers, embed_weight)
    gen_float = gen_emb.astype(jnp.float32)
    beam_float = beam_emb.astype(jnp.float32)
    gen_sq = jnp.sum(gen_float * gen_float, axis=1)
    beam_sq = jnp.sum(beam_float * beam_float, axis=1)
    rows = gen_emb.shape[0]
    columns = beam_emb.shape[0]
    log_beam = math.log(columns * lax.axis_size("beam"))
    log_gen = math.log(rows * lax.axis_size("gen"))
    beam_pot = jnp.zeros((columns,), jnp.float32)
    gen_pot = jnp.zeros((rows,), jnp.float32)
    for sweep in range(SWEEPS):
        temper = eps_roster[sweep]
        cost = tile_cost(gen_emb, beam_emb, gen_sq, beam_sq)
        gen_pot = temper * (log_beam - row_lse((beam_pot[None, :] - cost) / temper))
        cost = tile_cost(gen_emb, beam_emb, gen_sq, beam_sq)
        beam_pot = temper * (log_gen - col_lse((gen_pot[:, None] - cost) / temper))
    last = eps_roster[SWEEPS - 1]
    cost = tile_cost(gen_emb, beam_emb, gen_sq, beam_sq)
    mass = jnp.exp((gen_pot[:, None] + beam_pot[None, :] - cost) / last - log_beam)
    plan = mass.astype(jnp.bfloat16)
    gen_count = rows // lax.axis_size("beam")
    part = plan
    row_mass = jnp.sum(mass, axis=1)
    own = gen_float
    moved = jnp.dot(part, beam_emb, preferred_element_type=jnp.float32)
    grad_gen = lax.psum_scatter(
        2.0 * (row_mass[:, None] * own - moved), "beam", scatter_dimension=0, tiled=True
    )
    gen_start = lax.axis_index("beam") * gen_count
    act_rows = lax.dynamic_slice_in_dim(gen_act, gen_start, gen_count, 0)
    shower_rows = lax.dynamic_slice_in_dim(gen_showers, gen_start, gen_count, 0)
    beam_count = columns // lax.axis_size("gen")
    part = plan
    col_mass = jnp.sum(mass, axis=0)
    own = beam_float
    moved = lax.dot_general(
        part, gen_emb, (((0,), (0,)), ((), ())), preferred_element_type=jnp.float32
    )
    grad_beam = lax.psum_scatter(
        2.0 * (col_mass[:, None] * own - moved), "gen", scatter_dimension=0, tiled=True
    )
    beam_start = lax.axis_index("gen") * beam_count
    act_cols = lax.dynamic_slice_in_dim(beam_act, beam_start, beam_count, 0)
    shower_cols = lax.dynamic_slice_in_dim(beam_showers, beam_start, beam_count, 0)
    partial_grad = transpose_dot(shower_rows, grad_gen * (1.0 - act_rows * act_rows))
    partial_grad = partial_grad + transpose_dot(
        shower_cols, grad_beam * (1.0 - act_cols * act_cols)
    )
    weight_grad = lax.psum(partial_grad, ("gen", "beam"))
    return (gen_pot, beam_pot, weight_grad)


def solution(mesh):
    in_specs = (P("gen", None), P("beam", None), P(), P())
    out_specs = (P("gen"), P("beam"), P())
    return jax.shard_map(
        on_device, mesh=mesh, in_specs=in_specs, out_specs=out_specs, check_vma=False
    )
```

profile of v0, /device:TPU:8, one launch (start us, length us, event | category | flops | bytes accessed | tf_op | source)
XLA Modules:
  0.0 1114.6 jit_solution(14821040143072383777)
XLA Ops:
  11.4 5.3 fusion
  16.7 20.0 %pmax.56 = f32[1024]{0:T(1024)S(1)} all-reduce(f32[1024]{0:T(1024)S(1)} %get-tuple-element.16), channel_id=1, replica_groups=mesh['gen'=32,'beam'=8] {'beam'}, use_global_device_ids=true, to_apply=%region_3.0 | all-reduce | flops 1024 | bytes 8192 | tf_op jit(solution)/shard_map/pmax | solution.py:23
  36.7 5.1 exponential_reduce_fusion.7
  41.8 14.2 %psum.63 = f32[1024]{0:T(1024)S(1)} all-reduce(f32[1024]{0:T(1024)S(1)} %exponential_reduce_fusion.7), channel_id=1, replica_groups=mesh['gen'=32,'beam'=8] {'beam'}, use_global_device_ids=true, to_apply=%region_5.0 | all-reduce | flops 1024 | bytes 8192 | tf_op jit(solution)/shard_map/psum | solution.py:24
  61.3 54.0 %pmax.57 = f32[2048]{0:T(1024)S(1)} all-reduce(f32[2048]{0:T(1024)S(1)} %fusion.15), channel_id=1, replica_groups=mesh['gen'=32,'beam'=8] {'gen'}, use_global_device_ids=true, to_apply=%region_7.0 | all-reduce | flops 2048 | bytes 16384 | tf_op jit(solution)/shard_map/pmax | solution.py:29
  115.4 5.2 exponential_reduce_fusion.6
  120.5 55.5 %psum.64 = f32[2048]{0:T(1024)S(1)} all-reduce(f32[2048]{0:T(1024)S(1)} %exponential_reduce_fusion.6), channel_id=1, replica_groups=mesh['gen'=32,'beam'=8] {'gen'}, use_global_device_ids=true, to_apply=%region_9.0 | all-reduce | flops 2048 | bytes 16384 | tf_op jit(solution)/shard_map/psum | solution.py:30
  176.7 4.8 fusion.1
  181.5 16.2 %pmax.58 = f32[1024]{0:T(1024)S(1)} all-reduce(f32[1024]{0:T(1024)S(1)} %fusion.1), channel_id=1, replica_groups=mesh['gen'=32,'beam'=8] {'beam'}, use_global_device_ids=true, to_apply=%region_11.0 | all-reduce | flops 1024 | bytes 8192 | tf_op jit(solution)/shard_map/pmax | solution.py:23
  197.7 5.1 exponential_reduce_fusion.5
  202.8 14.2 %psum.65 = f32[1024]{0:T(1024)S(1)} all-reduce(f32[1024]{0:T(1024)S(1)} %exponential_reduce_fusion.5), channel_id=1, replica_groups=mesh['gen'=32,'beam'=8] {'beam'}, use_global_device_ids=true, to_apply=%region_13.0 | all-reduce | flops 1024 | bytes 8192 | tf_op jit(solution)/shard_map/psum | solution.py:24
  222.1 63.7 %pmax.59 = f32[2048]{0:T(1024)S(1)} all-reduce(f32[2048]{0:T(1024)S(1)} %fusion.16), channel_id=1, replica_groups=mesh['gen'=32,'beam'=8] {'gen'}, use_global_device_ids=true, to_apply=%region_15.0 | all-reduce | flops 2048 | bytes 16384 | tf_op jit(solution)/shard_map/pmax | solution.py:29
  285.8 5.1 exponential_reduce_fusion.4
  290.9 63.7 %psum.66 = f32[2048]{0:T(1024)S(1)} all-reduce(f32[2048]{0:T(1024)S(1)} %exponential_reduce_fusion.4), channel_id=1, replica_groups=mesh['gen'=32,'beam'=8] {'gen'}, use_global_device_ids=true, to_apply=%region_17.0 | all-reduce | flops 2048 | bytes 16384 | tf_op jit(solution)/shard_map/psum | solution.py:30
  355.2 4.9 fusion.2
  360.1 16.2 %pmax.60 = f32[1024]{0:T(1024)S(1)} all-reduce(f32[1024]{0:T(1024)S(1)} %fusion.2), channel_id=1, replica_groups=mesh['gen'=32,'beam'=8] {'beam'}, use_global_device_ids=true, to_apply=%region_19.0 | all-reduce | flops 1024 | bytes 8192 | tf_op jit(solution)/shard_map/pmax | solution.py:23
  376.3 5.1 exponential_reduce_fusion.3
  381.4 14.3 %psum.67 = f32[1024]{0:T(1024)S(1)} all-reduce(f32[1024]{0:T(1024)S(1)} %exponential_reduce_fusion.3), channel_id=1, replica_groups=mesh['gen'=32,'beam'=8] {'beam'}, use_global_device_ids=true, to_apply=%region_21.0 | all-reduce | flops 1024 | bytes 8192 | tf_op jit(solution)/shard_map/psum | solution.py:24
  401.1 63.7 %pmax.61 = f32[2048]{0:T(1024)S(1)} all-reduce(f32[2048]{0:T(1024)S(1)} %fusion.17), channel_id=1, replica_groups=mesh['gen'=32,'beam'=8] {'gen'}, use_global_device_ids=true, to_apply=%region_23.0 | all-reduce | flops 2048 | bytes 16384 | tf_op jit(solution)/shard_map/pmax | solution.py:29
  464.8 5.2 exponential_reduce_fusion.2
  470.0 63.7 %psum.68 = f32[2048]{0:T(1024)S(1)} all-reduce(f32[2048]{0:T(1024)S(1)} %exponential_reduce_fusion.2), channel_id=1, replica_groups=mesh['gen'=32,'beam'=8] {'gen'}, use_global_device_ids=true, to_apply=%region_25.0 | all-reduce | flops 2048 | bytes 16384 | tf_op jit(solution)/shard_map/psum | solution.py:30
  534.3 4.9 fusion.3
  539.2 16.2 %pmax.62 = f32[1024]{0:T(1024)S(1)} all-reduce(f32[1024]{0:T(1024)S(1)} %fusion.3), channel_id=1, replica_groups=mesh['gen'=32,'beam'=8] {'beam'}, use_global_device_ids=true, to_apply=%region_27.0 | all-reduce | flops 1024 | bytes 8192 | tf_op jit(solution)/shard_map/pmax | solution.py:23
  555.4 5.1 exponential_reduce_fusion.1
  560.5 14.2 %psum.69 = f32[1024]{0:T(1024)S(1)} all-reduce(f32[1024]{0:T(1024)S(1)} %exponential_reduce_fusion.1), channel_id=1, replica_groups=mesh['gen'=32,'beam'=8] {'beam'}, use_global_device_ids=true, to_apply=%region_29.0 | all-reduce | flops 1024 | bytes 8192 | tf_op jit(solution)/shard_map/psum | solution.py:24
  580.0 63.7 %pmax.63 = f32[2048]{0:T(1024)S(1)} all-reduce(f32[2048]{0:T(1024)S(1)} %fusion.18), channel_id=1, replica_groups=mesh['gen'=32,'beam'=8] {'gen'}, use_global_device_ids=true, to_apply=%region_31.0 | all-reduce | flops 2048 | bytes 16384 | tf_op jit(solution)/shard_map/pmax | solution.py:29
  643.7 5.2 exponential_reduce_fusion
  648.9 63.7 %psum.70 = f32[2048]{0:T(1024)S(1)} all-reduce(f32[2048]{0:T(1024)S(1)} %exponential_reduce_fusion), channel_id=1, replica_groups=mesh['gen'=32,'beam'=8] {'gen'}, use_global_device_ids=true, to_apply=%region_33.0 | all-reduce | flops 2048 | bytes 16384 | tf_op jit(solution)/shard_map/psum | solution.py:30
  713.3 5.7 fusion.37
  728.0 92.3 %reduce-scatter.5.cloned.1.call-done = f32[64,128]{1,0:T(8,128)} async-done(((f32[2048,128]{1,0:T(8,128)}), f32[64,128]{1,0:T(8,128)}) %reduce-scatter.5.cloned.1.call-update) | async-done | bytes 32784 | tf_op jit(solution)/shard_map/reduce_scatter | solution.py:85
  821.3 38.7 %reduce-scatter.3.cloned.1.call-done = f32[128,128]{0,1:T(8,128)} async-done(((f32[1024,128]{0,1:T(8,128)}), f32[128,128]{0,1:T(8,128)}) %reduce-scatter.3.cloned.1.call-update) | async-done | bytes 65552 | tf_op jit(solution)/shard_map/reduce_scatter | solution.py:72
  861.7 244.8 %all-reduce.2.cloned.1.call-done = f32[256,128]{1,0:T(8,128)} async-done(((f32[256,128]{1,0:T(8,128)}), f32[256,128]{1,0:T(8,128)}) %all-reduce.2.cloned.1.call-update) | async-done | bytes 131088 | tf_op jit(solution)/shard_map/psum | solution.py:95
  (34 shorter events, 41.2 us)
Async XLA Ops:
  7.2 1.5 copy-start
  7.2 813.0 %reduce-scatter.5.cloned.1.call-start = ((), (), s32[]{:S(2)}) async-start(), calls=%async_computation.3 | async-start | bytes 1081344 | tf_op jit(solution)/shard_map/reduce_scatter | solution.py:85
  575.4 137.9 %copy-start.2 = (f32[1024]{0:T(1024)}, f32[1024]{0:T(1024)S(1)}, u32[]{:S(2)}) copy-start(f32[1024]{0:T(1024)S(1)} %subtract_multiply_fusion.4) | copy-start | bytes 12292
  713.3 10.0 copy-start.3
  719.0 1.9 copy-start.1
  723.3 136.6 %reduce-scatter.3.cloned.1.call-start = ((), (), s32[]{:S(2)}) async-start(), calls=%async_computation.2 | async-start | bytes 589824 | tf_op jit(solution)/shard_map/reduce_scatter | solution.py:72
  727.9 378.6 %all-reduce.2.cloned.1.call-start = ((), (), s32[]{:S(2)}) async-start(), calls=%async_computation.4 | async-start | bytes 262144 | tf_op jit(solution)/shard_map/psum | solution.py:95
Sparse Core Ops, SparseCore 0:
  723.5 96.7 reduce-scatter.4
  822.9 36.9 reduce-scatter.2
  866.0 240.4 all-reduce.1
where the time goes:
time: 1120 us; the launch traced here: 1110 us
  blocking collectives  617 us (55%)
  waiting for transfers between devices  376 us (34%)
  other arithmetic  85 us (8%)
  matrix products  17.8 us (2%)
  between operations  14 us (1%)
    psum x4, blocking collectives, col_lse(): total = lax.psum(jnp.sum(jnp.exp(scores - top[None, :]), axis=0), 'gen')  247 us
    pmax x4, blocking collectives, col_lse(): top = lax.pmax(jnp.max(scores, axis=0), 'gen')  245 us
    psum x1, waiting for transfers between devices, on_device(): weight_grad = lax.psum(partial_grad, ('gen', 'beam'))  245 us
    reduce_scatter x1, waiting for transfers between devices, on_device(): lax.psum_scatter(2.0 * (col_mass[:, None] * own - moved), 'gen', scatter_...  92.3 us
    pmax x4, blocking collectives, row_lse(): top = lax.pmax(jnp.max(scores, axis=1), 'beam')  68.5 us
    psum x4, blocking collectives, row_lse(): total = lax.psum(jnp.sum(jnp.exp(scores - top[:, None]), axis=1), 'beam')  56.8 us
    reduce_scatter x1, waiting for transfers between devices, on_device(): lax.psum_scatter(2.0 * (row_mass[:, None] * own - moved), 'beam', scatter...  38.7 us
  transfers between devices with their start and end apart: 3, of which 3 were waited for; matrix products, arithmetic and copies ran while one was open for 0% of the time, Pallas kernels for 0%

commit v1 on v0

--- a/solution.py
+++ b/solution.py
@@ -92,7 +92,7 @@
     partial_grad = partial_grad + transpose_dot(
         shower_cols, grad_beam * (1.0 - act_cols * act_cols)
     )
-    weight_grad = lax.psum(partial_grad, ("gen", "beam"))
+    weight_grad = lax.psum(lax.psum(partial_grad, "gen"), "beam")
     return (gen_pot, beam_pot, weight_grad)
 
 

time: 1120 us -> 1060 us (0.946)
  waiting for transfers between devices: 376 us -> 315 us
    psum x1 -> x2, waiting for transfers between devices: 245 us -> 184 us  [on_device(): weight_grad = lax.psum(lax.psum(partial_grad, 'gen'), 'beam')]
  transfers between devices with their start and end apart: 3 -> 4, of which waited for: 3 -> 4; matrix products, arithmetic and copies ran while one was open for 0% -> 1% of each run, Pallas kernels for 0% -> 0%
where the time goes in v1:
time: 1060 us; the launch traced here: 1050 us
  blocking collectives  617 us (58%)
  waiting for transfers between devices  315 us (30%)
  other arithmetic  85 us (8%)
  matrix products  17.8 us (2%)
  between operations  14 us (1%)
    psum x4, blocking collectives, col_lse(): total = lax.psum(jnp.sum(jnp.exp(scores - top[None, :]), axis=0), 'gen')  247 us
    pmax x4, blocking collectives, col_lse(): top = lax.pmax(jnp.max(scores, axis=0), 'gen')  245 us
    psum x2, waiting for transfers between devices, on_device(): weight_grad = lax.psum(lax.psum(partial_grad, 'gen'), 'beam')  184 us
    reduce_scatter x1, waiting for transfers between devices, on_device(): lax.psum_scatter(2.0 * (col_mass[:, None] * own - moved), 'gen', scatter_...  92.3 us
    pmax x4, blocking collectives, row_lse(): top = lax.pmax(jnp.max(scores, axis=1), 'beam')  68.5 us
    psum x4, blocking collectives, row_lse(): total = lax.psum(jnp.sum(jnp.exp(scores - top[:, None]), axis=1), 'beam')  56.8 us
    reduce_scatter x1, waiting for transfers between devices, on_device(): lax.psum_scatter(2.0 * (row_mass[:, None] * own - moved), 'beam', scatter...  38.7 us
  transfers between devices with their start and end apart: 4, of which 4 were waited for; matrix products, arithmetic and copies ran while one was open for 1% of the time, Pallas kernels for 0%

profile of v1, /device:TPU:8, one launch (start us, length us, event | category | flops | bytes accessed | tf_op | source)
XLA Modules:
  0.0 1054.3 jit_solution(7304851526449598381)
XLA Ops:
  11.4 5.3 fusion
  16.7 20.0 %pmax.56 = f32[1024]{0:T(1024)S(1)} all-reduce(f32[1024]{0:T(1024)S(1)} %get-tuple-element.16), channel_id=1, replica_groups=mesh['gen'=32,'beam'=8] {'beam'}, use_global_device_ids=true, to_apply=%region_3.0 | all-reduce | flops 1024 | bytes 8192 | tf_op jit(solution)/shard_map/pmax | solution.py:23
  36.7 5.1 exponential_reduce_fusion.7
  41.8 14.2 %psum.70 = f32[1024]{0:T(1024)S(1)} all-reduce(f32[1024]{0:T(1024)S(1)} %exponential_reduce_fusion.7), channel_id=1, replica_groups=mesh['gen'=32,'beam'=8] {'beam'}, use_global_device_ids=true, to_apply=%region_5.0 | all-reduce | flops 1024 | bytes 8192 | tf_op jit(solution)/shard_map/psum | solution.py:24
  61.3 54.0 %pmax.57 = f32[2048]{0:T(1024)S(1)} all-reduce(f32[2048]{0:T(1024)S(1)} %fusion.15), channel_id=1, replica_groups=mesh['gen'=32,'beam'=8] {'gen'}, use_global_device_ids=true, to_apply=%region_7.0 | all-reduce | flops 2048 | bytes 16384 | tf_op jit(solution)/shard_map/pmax | solution.py:29
  115.4 5.2 exponential_reduce_fusion.6
  120.5 55.5 %psum.71 = f32[2048]{0:T(1024)S(1)} all-reduce(f32[2048]{0:T(1024)S(1)} %exponential_reduce_fusion.6), channel_id=1, replica_groups=mesh['gen'=32,'beam'=8] {'gen'}, use_global_device_ids=true, to_apply=%region_9.0 | all-reduce | flops 2048 | bytes 16384 | tf_op jit(solution)/shard_map/psum | solution.py:30
  181.5 16.2 %pmax.58 = f32[1024]{0:T(1024)S(1)} all-reduce(f32[1024]{0:T(1024)S(1)} %fusion.1), channel_id=1, replica_groups=mesh['gen'=32,'beam'=8] {'beam'}, use_global_device_ids=true, to_apply=%region_11.0 | all-reduce | flops 1024 | bytes 8192 | tf_op jit(solution)/shard_map/pmax | solution.py:23
  197.7 5.1 exponential_reduce_fusion.5
  202.8 14.2 %psum.72 = f32[1024]{0:T(1024)S(1)} all-reduce(f32[1024]{0:T(1024)S(1)} %exponential_reduce_fusion.5), channel_id=1, replica_groups=mesh['gen'=32,'beam'=8] {'beam'}, use_global_device_ids=true, to_apply=%region_13.0 | all-reduce | flops 1024 | bytes 8192 | tf_op jit(solution)/shard_map/psum | solution.py:24
  222.1 63.7 %pmax.59 = f32[2048]{0:T(1024)S(1)} all-reduce(f32[2048]{0:T(1024)S(1)} %fusion.16), channel_id=1, replica_groups=mesh['gen'=32,'beam'=8] {'gen'}, use_global_device_ids=true, to_apply=%region_15.0 | all-reduce | flops 2048 | bytes 16384 | tf_op jit(solution)/shard_map/pmax | solution.py:29
  285.8 5.1 exponential_reduce_fusion.4
  290.9 63.7 %psum.73 = f32[2048]{0:T(1024)S(1)} all-reduce(f32[2048]{0:T(1024)S(1)} %exponential_reduce_fusion.4), channel_id=1, replica_groups=mesh['gen'=32,'beam'=8] {'gen'}, use_global_device_ids=true, to_apply=%region_17.0 | all-reduce | flops 2048 | bytes 16384 | tf_op jit(solution)/shard_map/psum | solution.py:30
  355.2 4.9 fusion.2
  360.1 16.2 %pmax.60 = f32[1024]{0:T(1024)S(1)} all-reduce(f32[1024]{0:T(1024)S(1)} %fusion.2), channel_id=1, replica_groups=mesh['gen'=32,'beam'=8] {'beam'}, use_global_device_ids=true, to_apply=%region_19.0 | all-reduce | flops 1024 | bytes 8192 | tf_op jit(solution)/shard_map/pmax | solution.py:23
  376.3 5.1 exponential_reduce_fusion.3
  381.4 14.3 %psum.74 = f32[1024]{0:T(1024)S(1)} all-reduce(f32[1024]{0:T(1024)S(1)} %exponential_reduce_fusion.3), channel_id=1, replica_groups=mesh['gen'=32,'beam'=8] {'beam'}, use_global_device_ids=true, to_apply=%region_21.0 | all-reduce | flops 1024 | bytes 8192 | tf_op jit(solution)/shard_map/psum | solution.py:24
  401.1 63.7 %pmax.61 = f32[2048]{0:T(1024)S(1)} all-reduce(f32[2048]{0:T(1024)S(1)} %fusion.17), channel_id=1, replica_groups=mesh['gen'=32,'beam'=8] {'gen'}, use_global_device_ids=true, to_apply=%region_23.0 | all-reduce | flops 2048 | bytes 16384 | tf_op jit(solution)/shard_map/pmax | solution.py:29
  464.8 5.2 exponential_reduce_fusion.2
  470.0 63.7 %psum.75 = f32[2048]{0:T(1024)S(1)} all-reduce(f32[2048]{0:T(1024)S(1)} %exponential_reduce_fusion.2), channel_id=1, replica_groups=mesh['gen'=32,'beam'=8] {'gen'}, use_global_device_ids=true, to_apply=%region_25.0 | all-reduce | flops 2048 | bytes 16384 | tf_op jit(solution)/shard_map/psum | solution.py:30
  534.3 4.9 fusion.3
  539.2 16.2 %pmax.62 = f32[1024]{0:T(1024)S(1)} all-reduce(f32[1024]{0:T(1024)S(1)} %fusion.3), channel_id=1, replica_groups=mesh['gen'=32,'beam'=8] {'beam'}, use_global_device_ids=true, to_apply=%region_27.0 | all-reduce | flops 1024 | bytes 8192 | tf_op jit(solution)/shard_map/pmax | solution.py:23
  555.4 5.1 exponential_reduce_fusion.1
  560.5 14.2 %psum.76 = f32[1024]{0:T(1024)S(1)} all-reduce(f32[1024]{0:T(1024)S(1)} %exponential_reduce_fusion.1), channel_id=1, replica_groups=mesh['gen'=32,'beam'=8] {'beam'}, use_global_device_ids=true, to_apply=%region_29.0 | all-reduce | flops 1024 | bytes 8192 | tf_op jit(solution)/shard_map/psum | solution.py:24
  580.0 63.7 %pmax.63 = f32[2048]{0:T(1024)S(1)} all-reduce(f32[2048]{0:T(1024)S(1)} %fusion.18), channel_id=1, replica_groups=mesh['gen'=32,'beam'=8] {'gen'}, use_global_device_ids=true, to_apply=%region_31.0 | all-reduce | flops 2048 | bytes 16384 | tf_op jit(solution)/shard_map/pmax | solution.py:29
  643.7 5.2 exponential_reduce_fusion
  648.9 63.7 %psum.77 = f32[2048]{0:T(1024)S(1)} all-reduce(f32[2048]{0:T(1024)S(1)} %exponential_reduce_fusion), channel_id=1, replica_groups=mesh['gen'=32,'beam'=8] {'gen'}, use_global_device_ids=true, to_apply=%region_33.0 | all-reduce | flops 2048 | bytes 16384 | tf_op jit(solution)/shard_map/psum | solution.py:30
  713.3 5.7 fusion.37
  728.0 92.3 %reduce-scatter.5.cloned.1.call-done = f32[64,128]{1,0:T(8,128)} async-done(((f32[2048,128]{1,0:T(8,128)}), f32[64,128]{1,0:T(8,128)}) %reduce-scatter.5.cloned.1.call-update) | async-done | bytes 32784 | tf_op jit(solution)/shard_map/reduce_scatter | solution.py:85
  821.3 38.7 %reduce-scatter.3.cloned.1.call-done = f32[128,128]{0,1:T(8,128)} async-done(((f32[1024,128]{0,1:T(8,128)}), f32[128,128]{0,1:T(8,128)}) %reduce-scatter.3.cloned.1.call-update) | async-done | bytes 65552 | tf_op jit(solution)/shard_map/reduce_scatter | solution.py:72
  861.8 109.8 %all-reduce.3.cloned.1.call-done = f32[256,128]{1,0:T(8,128)} async-done(((f32[256,128]{1,0:T(8,128)}), f32[256,128]{1,0:T(8,128)}) %all-reduce.3.cloned.1.call-update) | async-done | bytes 131088 | tf_op jit(solution)/shard_map/psum | solution.py:95
  971.7 74.5 %all-reduce.5.cloned.1.call-done = f32[256,128]{1,0:T(8,128)} async-done(((f32[256,128]{1,0:T(8,128)}), f32[256,128]{1,0:T(8,128)}) %all-reduce.5.cloned.1.call-update) | async-done | bytes 131088 | tf_op jit(solution)/shard_map/psum | solution.py:95
  (37 shorter events, 46.1 us)
Async XLA Ops:
  7.2 1.5 copy-start
  7.2 813.0 %reduce-scatter.5.cloned.1.call-start = ((), (), s32[]{:S(2)}) async-start(), calls=%async_computation.3 | async-start | bytes 1081344 | tf_op jit(solution)/shard_map/reduce_scatter | solution.py:85
  575.4 137.9 %copy-start.2 = (f32[1024]{0:T(1024)}, f32[1024]{0:T(1024)S(1)}, u32[]{:S(2)}) copy-start(f32[1024]{0:T(1024)S(1)} %subtract_multiply_fusion.4) | copy-start | bytes 12292
  713.3 10.0 copy-start.3
  719.0 1.9 copy-start.1
  723.3 136.6 %reduce-scatter.3.cloned.1.call-start = ((), (), s32[]{:S(2)}) async-start(), calls=%async_computation.2 | async-start | bytes 589824 | tf_op jit(solution)/shard_map/reduce_scatter | solution.py:72
  727.9 243.7 %all-reduce.3.cloned.1.call-start = ((), (), s32[]{:S(2)}) async-start(), calls=%async_computation.4 | async-start | bytes 262144 | tf_op jit(solution)/shard_map/psum | solution.py:95
  861.7 184.5 %all-reduce.5.cloned.1.call-start = ((), (), s32[]{:S(2)}) async-start(), calls=%async_computation.5 | async-start | bytes 262144 | tf_op jit(solution)/shard_map/psum | solution.py:95
Sparse Core Ops, SparseCore 0:
  723.5 96.7 reduce-scatter.4
  822.9 36.9 reduce-scatter.2
  863.7 107.8 all-reduce.2
  973.9 72.2 all-reduce.4
